TPU v7x, 32 devices: a whole 2x2x4 slice. The times are simulated.
32 devices in a mesh: lon: 8 (over z, x), lat: 4 (over y, core).
Axes of the slice: x: 2, y: 2, z: 4, core: 2. Of those that a mesh axis runs over, the one named last changes fastest.
Arguments:
- thick: float32 [4, 768, 5760], P(None, 'lat', 'lon'), may hold values from 0.5 to 1.5
- uwind: float32 [4, 768, 5760], P(None, 'lat', 'lon'), may hold values from -3 to 3
- vwind: float32 [4, 768, 5760], P(None, 'lat', 'lon'), may hold values from -3 to 3
- theta: float32 [4, 768, 5760], P(None, 'lat', 'lon'), may hold values from -4 to 4
- moist: float32 [4, 768, 5760], P(None, 'lat', 'lon'), may hold values from -4 to 4
- lon_courant: float32 [768], P('lat'), may hold values from 0.05 to 0.5
- lat_courant: float32 [], replicated, may hold values from 0.2 to 0.5
- coriolis: float32 [768], P('lat'), may hold values from -0.5 to 0.5
- cap_mask: int32 [768], P('lat'), may hold values from 0 to 1, as said below
- cutoffs: int32 [768], P('lat'), may hold values from 1 to 255, as said below
Outputs:
- thick_new: float32 [4, 768, 5760], P(None, 'lat', 'lon')
- uwind_new: float32 [4, 768, 5760], P(None, 'lat', 'lon')
- vwind_new: float32 [4, 768, 5760], P(None, 'lat', 'lon')
- theta_mass: float32 [4, 768, 5760], P(None, 'lat', 'lon')
- moist_mass: float32 [4, 768, 5760], P(None, 'lat', 'lon')
Inputs may be any that keep to these rules, and one draw needn't show every extreme that they name: `cap_mask`: 0 on all rows outside the first 32 and the last 32 rows; the first and the last row hold 1. `cutoffs`: row 0 holds 255.
All inputs are finite; a program needn't handle non-finite values.
Results may differ from a plain program's by a relative error of at most 0.000098.
Values sent between devices are 32-bit elements; how exact they have to be, the bound alone decides.
A program may use at most 192 MiB of HBM per device.

v0:
```python
import functools
import math

import jax
import jax.numpy as jnp
import ml_dtypes
import numpy as np
from jax import lax
from jax.experimental import pallas as pl
from jax.experimental.pallas import tpu as pltpu
from jax.sharding import PartitionSpec as P

CAP = 32
KEEP = 256
RANK = 128
VMEM_LIMIT = 60 * 1024 * 1024


def split_table(table):
    table = np.asarray(table, np.float32)
    high = table.astype(ml_dtypes.bfloat16)
    low = (table - high.astype(np.float32)).astype(ml_dtypes.bfloat16)
    return high, low


@functools.lru_cache(maxsize=None)
def tables(cells, count, padded):
    full = cells * count
    t = np.arange(cells)
    band = (KEEP - 0.5) / full
    diag = ((cells - 1 - 2 * t) / 2.0) ** 2 * math.cos(2 * math.pi * band)
    off = t[1:] * (cells - t[1:]) / 2.0
    _, vectors = np.linalg.eigh(np.diag(diag) + np.diag(off, 1) + np.diag(off, -1))
    basis = vectors[:, ::-1][:, :RANK]
    basis = basis * np.where(basis[cells // 2 - 3] < 0, -1.0, 1.0)
    modes = np.arange(KEEP)
    blocks = []
    for s in range(count):
        phase = 2 * np.pi * (((s * cells + t)[:, None] * modes[None, :]) % full) / full
        blocks.append(basis.T @ np.concatenate([np.cos(phase), np.sin(phase)], 1))
    wide = np.zeros((padded, RANK))
    wide[:cells] = basis
    return split_table(wide) + split_table(wide.T) + split_table(np.concatenate(blocks, 0))


def halves(x):
    high = x.astype(jnp.bfloat16)
    return high, (x - high.astype(jnp.float32)).astype(jnp.bfloat16)


def dot3(x, high, low, rhs_dim=0):
    dims = (((1,), (rhs_dim,)), ((), ()))
    xh, xl = halves(x)
    dot = functools.partial(
        lax.dot_general, dimension_numbers=dims, preferred_element_type=jnp.float32
    )
    return dot(xh, high) + (dot(xl, high) + dot(xh, low))


def row_ids(width):
    return lax.broadcasted_iota(jnp.int32, (8, width), 0)


def row_up(cur, nxt, k, rows):
    return pltpu.roll(jnp.where(rows < k, nxt, cur), 8 - k, 0)


def row_down(cur, prv, k, rows):
    return pltpu.roll(jnp.where(rows >= 8 - k, prv, cur), k, 0)


def lane(x, k):
    return pltpu.roll(x, (-k) % x.shape[1], 1)


def face_terms(speed):
    part = speed * (1.0 / 12.0)
    seven = 7.0 * part
    half = 0.5 * jnp.abs(speed)
    return seven + half, seven - half, part


def lat_flux(load, r, b, masses, rows):
    v, vn = load(2, r), load(2, r + 8)
    p, q, s = face_terms((0.5 * b) * (v + row_up(v, vn, 1, rows)))
    out = []
    for m in masses:
        prv, cur, nxt = load(m, r - 8), load(m, r), load(m, r + 8)
        out.append(
            p * cur
            + q * row_up(cur, nxt, 1, rows)
            - s * (row_down(cur, prv, 1, rows) + row_up(cur, nxt, 2, rows))
        )
    return out


def chunk(load, r, a, f, b, masses, carry, rows):
    h, u, v = load(0, r), load(1, r), load(2, r)
    ue, uw = lane(u, 1), lane(u, -1)
    p, q, s = face_terms((0.5 * a) * (u + ue))
    fluxes = lat_flux(load, r, b, masses, rows)
    tends = []
    dh = None
    for m, up, before in zip(masses, fluxes, carry):
        cur = load(m, r)
        east, west = lane(cur, 1), lane(cur, -1)
        if m == 0:
            dh = east - west
        flux = p * cur + q * east - s * (west + lane(cur, 2))
        tends.append(lane(flux, -1) - flux + (row_down(up, before, 1, rows) - up))
    au, bv = (0.5 * a) * u, (0.5 * b) * v

    def across(m):
        prv, cur, nxt = load(m, r - 8), load(m, r), load(m, r + 8)
        return row_up(cur, nxt, 1, rows) - row_down(cur, prv, 1, rows)

    tend_u = f * v - au * (ue - uw) - bv * across(1) - (0.5 * a) * dh
    tend_v = (
        -(f * u) - au * (lane(v, 1) - lane(v, -1)) - bv * across(2) - (0.5 * b) * across(0)
    )
    return tends, tend_u, tend_v, fluxes


def widen(x, width, east, west, east_shift, west_shift):
    cells = x.shape[1]
    last = width - 128
    tail = jnp.concatenate(
        [x[:, last:], jnp.zeros((x.shape[0], width - cells), jnp.float32)], 1
    )
    ids = lax.broadcasted_iota(jnp.int32, (x.shape[0], 128), 1)
    e = cells - last
    tail = jnp.where((ids >= e) & (ids < e + 2), pltpu.roll(east, east_shift, 1), tail)
    tail = jnp.where(ids >= 126, pltpu.roll(west, west_shift, 1), tail)
    return x[:, :last], tail


def exchange_kernel(geo, *refs):
    lev, n_rows, cells, width, count, bands = geo
    left, right = refs[0:5], refs[5:10]
    fields = refs[10:15]
    par, lat_c, cuts, uh, ul, gh, gl = refs[15:22]
    out_east, out_west, out_north, out_south, out_coef = refs[22:27]
    (
        send_w, send_e, got_e, got_w, edge_n, edge_s, send_n, send_s, got_n, got_s,
        cap_raw, cap, cap_t, comp, mid_in, mid_out, coef,
        in_sem, lon_send, lon_recv, lat_send, lat_recv, a_send, a_recv, b_send, b_recv,
    ) = refs[27:]
    me = lax.axis_index("lon")
    band = lax.axis_index("lat")
    has_n = band > 0
    has_s = band < bands - 1
    is_cap = jnp.logical_or(band == 0, band == bands - 1)
    last = width - 128
    e = cells - last
    owned = 3 * lev * CAP // count

    barrier = pltpu.get_barrier_semaphore()
    for j in range(1, count):
        pl.semaphore_signal(barrier, inc=1, device_id={"lon": lax.rem(me + j, count)})

    @pl.when(has_n)
    def _():
        pl.semaphore_signal(barrier, inc=1, device_id={"lat": band - 1})

    @pl.when(has_s)
    def _():
        pl.semaphore_signal(barrier, inc=1, device_id={"lat": band + 1})

    cap_row = jnp.where(band == 0, 0, n_rows - CAP - 8)
    loads = []
    for k in range(5):
        loads.append(
            pltpu.make_async_copy(fields[k].at[:, pl.ds(0, 8), :], edge_n.at[k], in_sem.at[k])
        )
        loads.append(
            pltpu.make_async_copy(
                fields[k].at[:, pl.ds(n_rows - 8, 8), :], edge_s.at[k], in_sem.at[5 + k]
            )
        )
    cap_loads = [
        pltpu.make_async_copy(
            fields[k].at[:, pl.ds(pl.multiple_of(cap_row, 8), CAP + 8), :],
            cap_raw.at[k],
            in_sem.at[10 + k],
        )
        for k in range(3)
    ]
    for copy in loads + cap_loads:
        copy.start()

    ids = lax.broadcasted_iota(jnp.int32, (n_rows, 128), 1)
    west_edge = jnp.zeros((n_rows, 128), jnp.float32)
    east_edge = jnp.zeros((n_rows, 128), jnp.float32)
    for k in range(5):
        for level in range(lev):
            at = 2 * (5 * level + k)
            here = (ids >= at) & (ids < at + 2)
            west_edge = jnp.where(here, pltpu.roll(left[k][level], at, 1), west_edge)
            east_edge = jnp.where(
                here, pltpu.roll(right[k][level], (at - (e - 2)) % 128, 1), east_edge
            )
    send_w[...] = west_edge
    send_e[...] = east_edge

    greeted = count - 1 + jnp.where(has_n, 1, 0) + jnp.where(has_s, 1, 0)
    pl.semaphore_wait(barrier, greeted)

    to_west = pltpu.make_async_remote_copy(
        src_ref=send_w, dst_ref=got_e, send_sem=lon_send.at[0], recv_sem=lon_recv.at[0],
        device_id={"lon": lax.rem(me + count - 1, count)},
    )
    to_east = pltpu.make_async_remote_copy(
        src_ref=send_e, dst_ref=got_w, send_sem=lon_send.at[1], recv_sem=lon_recv.at[1],
        device_id={"lon": lax.rem(me + 1, count)},
    )
    to_west.start()
    to_east.start()

    for copy in loads:
        copy.wait()
    for k in range(5):
        for level in range(lev):
            send_n[level, 2 * k : 2 * k + 2, :] = edge_n[k, level, 0:2, :]
            send_s[level, 2 * k : 2 * k + 2, :] = edge_s[k, level, 6:8, :]
    to_north = pltpu.make_async_remote_copy(
        src_ref=send_n, dst_ref=got_s, send_sem=lat_send.at[0], recv_sem=lat_recv.at[0],
        device_id={"lat": lax.rem(band + bands - 1, bands)},
    )
    to_south = pltpu.make_async_remote_copy(
        src_ref=send_s, dst_ref=got_n, send_sem=lat_send.at[1], recv_sem=lat_recv.at[1],
        device_id={"lat": lax.rem(band + 1, bands)},
    )

    @pl.when(has_n)
    def _():
        to_north.start()

    @pl.when(has_s)
    def _():
        to_south.start()

    for copy in cap_loads:
        copy.wait()
    to_west.wait()
    to_east.wait()
    out_east[...] = got_e[...]
    out_west[...] = got_w[...]

    @pl.when(is_cap)
    def _():
        rows = row_ids(width)
        b = lat_c[0]
        halo_row = pl.multiple_of(cap_row, 8)
        for k in range(3):
            for level in range(lev):
                at = 2 * (5 * level + k)
                body, tail = widen(
                    cap_raw[k, level], width,
                    got_e[pl.ds(halo_row, CAP + 8), :], got_w[pl.ds(halo_row, CAP + 8), :],
                    (e - at) % 128, (126 - at) % 128,
                )
                cap[k, level, 0:8, :] = jnp.zeros((8, width), jnp.float32)
                cap[k, level, 8 : CAP + 16, :last] = body
                cap[k, level, 8 : CAP + 16, last:] = tail
                cap[k, level, CAP + 16 : CAP + 24, :] = jnp.zeros((8, width), jnp.float32)
        first = jnp.where(band == 0, 8, 16)

        def level_body(level, _):
            def load(m, r):
                return cap[m, level, pl.ds(pl.multiple_of(r, 8), 8), :]

            def body(c, carry):
                r = first + 8 * c
                pr = pl.multiple_of(jnp.where(band == 0, 0, n_rows - CAP) + 8 * c, 8)
                a = par[pl.ds(pr, 8), 0:1]
                f = par[pl.ds(pr, 8), 1:2]
                tends, tu, tv, fluxes = chunk(load, r, a, f, b, (0,), carry, rows)
                dst = pl.multiple_of(8 * c, 8)
                cap_t[0, level, pl.ds(dst, 8), :] = tends[0]
                cap_t[1, level, pl.ds(dst, 8), :] = tu
                cap_t[2, level, pl.ds(dst, 8), :] = tv
                return fluxes

            v, vn = load(2, first - 8), load(2, first)
            p, q, s = face_terms((0.5 * b) * (v + row_up(v, vn, 1, rows)))
            cur, nxt = load(0, first - 8), load(0, first)
            before = (
                p * cur
                + q * row_up(cur, nxt, 1, rows)
                - s * (row_down(cur, cur, 1, rows) + row_up(cur, nxt, 2, rows))
            )
            lax.fori_loop(0, CAP // 8, body, [before])
            return 0

        lax.fori_loop(0, lev, level_body, 0)
        flat = cap_t[...].reshape(3 * lev * CAP, width)
        comp[...] = dot3(flat, uh[...], ul[...]).reshape(count, owned, RANK)

        def send(src, dst, sends, recvs, j):
            peer = lax.rem(me + j, count)
            return pltpu.make_async_remote_copy(
                src_ref=src.at[peer], dst_ref=dst.at[me],
                send_sem=sends.at[j], recv_sem=recvs.at[j], device_id={"lon": peer},
            )

        first_sends = [send(comp, mid_in, a_send, a_recv, j) for j in range(1, count)]
        for copy in first_sends:
            copy.start()
        mid_in[me] = comp[me]
        for copy in first_sends:
            copy.wait()
        spectra = None
        for s in range(count):
            part = pl.ds(s * RANK, RANK)
            term = dot3(mid_in[s], gh[part, :], gl[part, :])
            spectra = term if spectra is None else spectra + term
        modes = lax.broadcasted_iota(jnp.int32, (owned, 2 * KEEP), 1)
        modes = jnp.where(modes >= KEEP, modes - KEEP, modes)
        full = cells * count
        weight = jnp.where(modes == 0, 1.0 / full, 2.0 / full).astype(jnp.float32)
        limit = cuts[pl.ds(pl.multiple_of(me * owned, 8), owned), 0:1]
        spectra = jnp.where(modes.astype(jnp.float32) <= limit, spectra * weight, 0.0)
        for s in range(count):
            part = pl.ds(s * RANK, RANK)
            mid_out[s] = dot3(spectra, gh[part, :], gl[part, :], 1)
        second_sends = [send(mid_out, coef, b_send, b_recv, j) for j in range(1, count)]
        for copy in second_sends:
            copy.start()
        coef[me] = mid_out[me]
        for copy in second_sends:
            copy.wait()
        out_coef[...] = coef[...].reshape(3 * lev * CAP, RANK)

    @pl.when(jnp.logical_not(is_cap))
    def _():
        out_coef[...] = jnp.zeros((3 * lev * CAP, RANK), jnp.float32)

    @pl.when(has_n)
    def _():
        to_north.wait_send()
        to_south_in = to_south
        to_south_in.wait_recv()
        out_north[...] = got_n[...]

    @pl.when(has_s)
    def _():
        to_south.wait_send()
        to_north.wait_recv()
        out_south[...] = got_s[...]

    @pl.when(jnp.logical_not(has_n))
    def _():
        out_north[...] = jnp.zeros(out_north.shape, jnp.float32)

    @pl.when(jnp.logical_not(has_s))
    def _():
        out_south[...] = jnp.zeros(out_south.shape, jnp.float32)


def step_kernel(geo, *refs):
    lev, n_rows, cells, width, count, bands = geo
    fields = refs[0:5]
    par, lat_c, east, west, north, south, coef, wh, wl = refs[5:14]
    outs = refs[14:19]
    pad = refs[19]
    level = pl.program_id(0)
    band = lax.axis_index("lat")
    last = width - 128
    e = cells - last
    rows = row_ids(width)
    b = lat_c[0]
    for k in range(5):
        pad[k, 0:8, :] = jnp.zeros((8, width), jnp.float32)
        pad[k, n_rows + 8 : n_rows + 16, :] = jnp.zeros((8, width), jnp.float32)
        pad[k, 6:8, :cells] = north[0, 2 * k : 2 * k + 2, :]
        pad[k, n_rows + 8 : n_rows + 10, :cells] = south[0, 2 * k : 2 * k + 2, :]
    for k in (3, 4):
        for r in (0, n_rows + 8):
            pad[k, r : r + 8, :] = pad[k, r : r + 8, :] * pad[0, r : r + 8, :]

    def fill(c, _):
        r = pl.multiple_of(8 * c, 8)
        to = pl.multiple_of(8 * c + 8, 8)
        ea, we = east[pl.ds(r, 8), :], west[pl.ds(r, 8), :]
        thick = None
        for k in range(5):
            at = 2 * (5 * level + k)
            body, tail = widen(
                fields[k][0, pl.ds(r, 8), :], width, ea, we,
                e + 128 - at, 126 - at,
            )
            if k == 0:
                thick = body, tail
            if k >= 3:
                body, tail = body * thick[0], tail * thick[1]
            pad[k, pl.ds(to, 8), :last] = body
            pad[k, pl.ds(to, 8), last:] = tail
        return 0

    lax.fori_loop(0, n_rows // 8, fill, 0)

    def load(m, r):
        return pad[m, pl.ds(pl.multiple_of(r, 8), 8), :]

    masses = (0, 3, 4)
    v, vn = load(2, 0), load(2, 8)
    p, q, s = face_terms((0.5 * b) * (v + row_up(v, vn, 1, rows)))
    before = []
    for m in masses:
        cur, nxt = load(m, 0), load(m, 8)
        before.append(
            p * cur
            + q * row_up(cur, nxt, 1, rows)
            - s * (row_down(cur, cur, 1, rows) + row_up(cur, nxt, 2, rows))
        )

    def body(c, carry):
        r = 8 * c + 8
        src = pl.multiple_of(8 * c, 8)
        a = par[pl.ds(src, 8), 0:1]
        f = par[pl.ds(src, 8), 1:2]
        tends, tu, tv, fluxes = chunk(load, r, a, f, b, masses, carry, rows)
        for k, t in zip(range(5), (tends[0], tu, tv, tends[1], tends[2])):
            outs[k][0, pl.ds(src, 8), :] = (load(k, r) + t)[:, :cells]
        return fluxes

    lax.fori_loop(0, n_rows // 8, body, before)

    @pl.when(jnp.logical_or(band == 0, band == bands - 1))
    def _():
        start = pl.multiple_of(jnp.where(band == 0, 0, n_rows - CAP), 8)
        flat = coef[...].reshape(3 * CAP, RANK)
        smooth = dot3(flat, wh[...], wl[...])
        chosen = par[pl.ds(start, CAP), 2:3] == 1.0
        for k in range(3):
            new = fields[k][0, pl.ds(start, CAP), :] + smooth[CAP * k : CAP * k + CAP, :cells]
            old = outs[k][0, pl.ds(start, CAP), :]
            outs[k][0, pl.ds(start, CAP), :] = jnp.where(chosen, new, old)


def local(thick, uwind, vwind, theta, moist, lon_courant, lat_courant, coriolis, cap_mask, cutoffs):
    lev, n_rows, cells = thick.shape
    count = lax.axis_size("lon")
    bands = lax.axis_size("lat")
    width = (cells + 4 + 127) // 128 * 128
    geo = (lev, n_rows, cells, width, count, bands)
    uh, ul, wh, wl, gh, gl = (jnp.asarray(t) for t in tables(cells, count, width))
    fields = (thick, uwind, vwind, theta, moist)
    par = jnp.stack(
        [lon_courant, coriolis, (cap_mask == 1).astype(jnp.float32)], 1
    )
    cap_cuts = jnp.where(
        lax.axis_index("lat") == 0, cutoffs[:CAP], cutoffs[n_rows - CAP :]
    ).astype(jnp.float32)
    cuts = jnp.tile(cap_cuts, 3 * lev)[:, None]
    lat_c = lat_courant.reshape(1)

    whole = lambda shape: pl.BlockSpec(shape, lambda i: (0,) * len(shape))
    smem = pl.BlockSpec(memory_space=pltpu.SMEM)
    edge = lambda col: pl.BlockSpec((lev, n_rows, 128), lambda i: (0, 0, col))
    owned = 3 * lev * CAP // count
    f32 = jnp.float32
    rows_all = 3 * lev * CAP
    dma = pltpu.SemaphoreType.DMA
    east, west, north, south, coef = pl.pallas_call(
        functools.partial(exchange_kernel, geo),
        grid=(1,),
        out_shape=(
            jax.ShapeDtypeStruct((n_rows, 128), f32),
            jax.ShapeDtypeStruct((n_rows, 128), f32),
            jax.ShapeDtypeStruct((lev, 10, cells), f32),
            jax.ShapeDtypeStruct((lev, 10, cells), f32),
            jax.ShapeDtypeStruct((rows_all, RANK), f32),
        ),
        in_specs=[edge(0)] * 5
        + [edge(cells // 128)] * 5
        + [pl.BlockSpec(memory_space=pl.ANY)] * 5
        + [whole(par.shape), smem, whole(cuts.shape)]
        + [whole(t.shape) for t in (uh, ul, gh, gl)],
        out_specs=(
            whole((n_rows, 128)),
            whole((n_rows, 128)),
            whole((lev, 10, cells)),
            whole((lev, 10, cells)),
            whole((rows_all, RANK)),
        ),
        scratch_shapes=[pltpu.VMEM((n_rows, 128), f32)] * 4
        + [pltpu.VMEM((5, lev, 8, cells), f32)] * 2
        + [pltpu.VMEM((lev, 10, cells), f32)] * 4
        + [
            pltpu.VMEM((3, lev, CAP + 8, cells), f32),
            pltpu.VMEM((3, lev, CAP + 24, width), f32),
            pltpu.VMEM((3, lev, CAP, width), f32),
        ]
        + [pltpu.VMEM((count, owned, RANK), f32)] * 4
        + [dma((13,))]
        + [dma((2,))] * 4
        + [dma((count,))] * 4,
        compiler_params=pltpu.CompilerParams(
            collective_id=0, has_side_effects=True, vmem_limit_bytes=VMEM_LIMIT
        ),
        name="exchange",
    )(*fields, *fields, *fields, par, lat_c, cuts, uh, ul, gh, gl)

    by_level = lambda shape: pl.BlockSpec(
        (1,) + shape, lambda i: (i,) + (0,) * len(shape)
    )
    coef = coef.reshape(3, lev, CAP, RANK)
    return pl.pallas_call(
        functools.partial(step_kernel, geo),
        grid=(lev,),
        out_shape=tuple(jax.ShapeDtypeStruct((lev, n_rows, cells), f32) for _ in range(5)),
        in_specs=[by_level((n_rows, cells))] * 5
        + [whole(par.shape), smem, whole((n_rows, 128)), whole((n_rows, 128))]
        + [by_level((10, cells))] * 2
        + [pl.BlockSpec((3, 1, CAP, RANK), lambda i: (0, i, 0, 0))]
        + [whole(wh.shape)] * 2,
        out_specs=[by_level((n_rows, cells))] * 5,
        scratch_shapes=[pltpu.VMEM((5, n_rows + 16, width), f32)],
        compiler_params=pltpu.CompilerParams(vmem_limit_bytes=VMEM_LIMIT),
        name="substep",
    )(*fields, par, lat_c, east, west, north, south, coef, wh, wl)


def solution(mesh):
    field = P(None, "lat", "lon")
    row = P("lat")
    return jax.shard_map(
        local,
        mesh=mesh,
        in_specs=(field,) * 5 + (row, P(), row, row, row),
        out_specs=(field,) * 5,
        check_vma=False,
    )
```

profile of v0, /device:TPU:0, one launch (start us, length us, event | category | flops | bytes accessed | tf_op | source)
XLA Modules:
  0.0 71.1 jit_solution(14770917239206111993)
XLA Ops:
  1.3 0.8 %fusion = f32[32]{0:T(128)S(1)} fusion(pred[]{:T(512)S(6)} %eq.11, s32[192]{0:T(256)} %param.25), kind=kLoop, calls=%fused_computation.3 | loop fusion | flops 64 | bytes 385 | tf_op jit(solution)/shard_map/convert_element_type | solution.py:454
  2.1 0.7 compare_convert_fusion
  2.8 0.7 pad_maximum_fusion
  3.5 0.8 %copy.27.refs_15_.refs_5_ = f32[192,3]{1,0:T(8,128)} copy(f32[192,3]{0,1:T(4,128)S(1)} %pad_maximum_fusion) | data formatting | bytes 4608 | tf_op jit(solution)/shard_map/stack | solution.py:449
  4.3 0.9 %broadcast_in_dim_tile.4.refs_17_ = f32[384,1]{1,0:T(8,128)} reshape(f32[12,32]{1,0:T(8,128)S(1)} %tile.2) | data formatting | bytes 3072 | tf_op jit(solution)/shard_map/broadcast_in_dim;tile | solution.py:455
  5.1 31.5 %exchange.1 = (f32[192,128]{1,0:T(8,128)}, f32[192,128]{1,0:T(8,128)}, f32[4,10,720]{2,1,0:T(8,128)}, f32[4,10,720]{2,1,0:T(8,128)}, f32[384,128]{1,0:T(8,128)}) custom-call(f32[4,192,720]{2,1,0:T(8,128)} %refs_0_.3, f32[4,192,720]{2,1,0:T(8,128)} %refs_1_.3, f32[4,192,720]{2,1,0:T(8,128)} %refs_2_.3, f32[4,192,720]{2,1,0:T(8,128)} %refs_3_.3, ...), custom_call_target="tpu_custom_call" | custom-call | tf_op jit(solution)/shard_map/exchange/pallas_call | solution.py:465
  36.6 34.5 %substep.1 = (f32[4,192,720]{2,1,0:T(8,128)}, f32[4,192,720]{2,1,0:T(8,128)}, f32[4,192,720]{2,1,0:T(8,128)}, f32[4,192,720]{2,1,0:T(8,128)}, f32[4,192,720]{2,1,0:T(8,128)}) custom-call(f32[4,192,720]{2,1,0:T(8,128)} %refs_0_.3, f32[4,192,720]{2,1,0:T(8,128)} %refs_1_.3, f32[4,192,720]{2,1,0:T(8,128)} %refs_2_.3, f32[4,192,720]{2,1,0:T(8,128)} %refs_3_.3, ...), custom_call_target="tpu_custom_call" | custom-call | tf_op jit(solution)/shard_map/substep/pallas_call | solution.py:509
  (1 shorter events, 0.0 us)
where the time goes:
time: 71.4 us; the launch traced here: 71.1 us
  Pallas kernels  66 us (92%)
  other arithmetic  2.21 us (3%)
  local copies, waits for them, and re-layouts  1.64 us (2%)
  between operations  1.3 us (2%)
    pallas_call x1, Pallas kernels, local(): pl.pallas_call(functools.partial(step_kernel, geo), grid=(lev,), out_shap...  34.5 us
    pallas_call x1, Pallas kernels, local(): pl.pallas_call(functools.partial(exchange_kernel, geo), grid=(1,), out_sh...  31.5 us

commit v1 on v0

--- a/solution.py
+++ b/solution.py
@@ -40,7 +40,10 @@
         blocks.append(basis.T @ np.concatenate([np.cos(phase), np.sin(phase)], 1))
     wide = np.zeros((padded, RANK))
     wide[:cells] = basis
-    return split_table(wide) + split_table(wide.T) + split_table(np.concatenate(blocks, 0))
+    modal = np.concatenate(blocks, 0)
+    return (
+        split_table(wide) + split_table(wide.T) + split_table(modal) + split_table(modal.T)
+    )
 
 
 def halves(x):
@@ -48,17 +51,19 @@
     return high, (x - high.astype(jnp.float32)).astype(jnp.bfloat16)
 
 
-def dot3(x, high, low, rhs_dim=0):
-    dims = (((1,), (rhs_dim,)), ((), ()))
+def dot3(x, high, low):
+    dot = functools.partial(jnp.dot, preferred_element_type=jnp.float32)
     xh, xl = halves(x)
-    dot = functools.partial(
-        lax.dot_general, dimension_numbers=dims, preferred_element_type=jnp.float32
-    )
-    return dot(xh, high) + (dot(xl, high) + dot(xh, low))
-
-
-def row_ids(width):
-    return lax.broadcasted_iota(jnp.int32, (8, width), 0)
+    rows = x.shape[0]
+    both = dot(jnp.concatenate([xh, xl], 0), high)
+    return both[:rows] + (both[rows:] + dot(xh, low))
+
+
+def eight_rows(vector, first, rows):
+    out = jnp.full(rows.shape, vector[first])
+    for k in range(1, 8):
+        out = jnp.where(rows == k, vector[first + k], out)
+    return out
 
 
 def row_up(cur, nxt, k, rows):
@@ -69,8 +74,19 @@
     return pltpu.roll(jnp.where(rows >= 8 - k, prv, cur), k, 0)
 
 
-def lane(x, k):
-    return pltpu.roll(x, (-k) % x.shape[1], 1)
+def lane_up(cur, nxt, k, lanes):
+    return pltpu.roll(jnp.where(lanes < k, nxt, cur), 128 - k, 1)
+
+
+def lane_down(cur, prv, k, lanes):
+    return pltpu.roll(jnp.where(lanes >= 128 - k, prv, cur), k, 1)
+
+
+def tile_ids():
+    return (
+        lax.broadcasted_iota(jnp.int32, (8, 128), 0),
+        lax.broadcasted_iota(jnp.int32, (8, 128), 1),
+    )
 
 
 def face_terms(speed):
@@ -80,45 +96,85 @@
     return seven + half, seven - half, part
 
 
-def lat_flux(load, r, b, masses, rows):
-    v, vn = load(2, r), load(2, r + 8)
-    p, q, s = face_terms((0.5 * b) * (v + row_up(v, vn, 1, rows)))
+def first_carry(load, r, b, masses, tiles, carry):
+    rows, _ = tile_ids()
+    for c in range(tiles):
+        v, vn = load(2, r, c), load(2, r + 8, c)
+        p, q, s = face_terms((0.5 * b) * (v + row_up(v, vn, 1, rows)))
+        for k, m in enumerate(masses):
+            cur, nxt = load(m, r, c), load(m, r + 8, c)
+            carry[k, :, 128 * c : 128 * c + 128] = (
+                p * cur
+                + q * row_up(cur, nxt, 1, rows)
+                - s * (row_down(cur, cur, 1, rows) + row_up(cur, nxt, 2, rows))
+            )
+
+
+def rolled(load, tiles):
+    lanes = tile_ids()[1]
+
+    def near(m, r, c, k):
+        cur = load(m, r, c)
+        if k > 0:
+            return lane_up(cur, load(m, r, (c + 1) % tiles), k, lanes)
+        return lane_down(cur, load(m, r, (c + tiles - 1) % tiles), -k, lanes)
+
+    return near
+
+
+def shift_tables():
+    eye = np.eye(128)
     out = []
-    for m in masses:
-        prv, cur, nxt = load(m, r - 8), load(m, r), load(m, r + 8)
-        out.append(
-            p * cur
-            + q * row_up(cur, nxt, 1, rows)
-            - s * (row_down(cur, prv, 1, rows) + row_up(cur, nxt, 2, rows))
-        )
-    return out
-
-
-def chunk(load, r, a, f, b, masses, carry, rows):
-    h, u, v = load(0, r), load(1, r), load(2, r)
-    ue, uw = lane(u, 1), lane(u, -1)
-    p, q, s = face_terms((0.5 * a) * (u + ue))
-    fluxes = lat_flux(load, r, b, masses, rows)
-    tends = []
-    dh = None
-    for m, up, before in zip(masses, fluxes, carry):
-        cur = load(m, r)
-        east, west = lane(cur, 1), lane(cur, -1)
-        if m == 0:
-            dh = east - west
-        flux = p * cur + q * east - s * (west + lane(cur, 2))
-        tends.append(lane(flux, -1) - flux + (row_down(up, before, 1, rows) - up))
-    au, bv = (0.5 * a) * u, (0.5 * b) * v
-
-    def across(m):
-        prv, cur, nxt = load(m, r - 8), load(m, r), load(m, r + 8)
-        return row_up(cur, nxt, 1, rows) - row_down(cur, prv, 1, rows)
-
-    tend_u = f * v - au * (ue - uw) - bv * across(1) - (0.5 * a) * dh
-    tend_v = (
-        -(f * u) - au * (lane(v, 1) - lane(v, -1)) - bv * across(2) - (0.5 * b) * across(0)
-    )
-    return tends, tend_u, tend_v, fluxes
+    for pair in ((1, 2), (1, -1)):
+        moves = np.concatenate([np.roll(eye, -k, 0).T for k in pair], 1)
+        out.append(np.concatenate([moves, moves], 0).astype(ml_dtypes.bfloat16))
+    return np.stack(out)
+
+
+def chunk(load, near, r, a, f, b, masses, tiles, carry, emit):
+    rows, lanes = tile_ids()
+    half_a = 0.5 * a
+
+    def lon_part(c):
+        ue = near(1, r, c, 1)
+        p, q, s = face_terms(half_a * (load(1, r, c) + ue))
+        fluxes, dh = [], None
+        for m in masses:
+            e, w = near(m, r, c, 1), near(m, r, c, -1)
+            if m == 0:
+                dh = e - w
+            fluxes.append(p * load(m, r, c) + q * e - s * (w + near(m, r, c, 2)))
+        return fluxes, dh, ue
+
+    wrapped = lon_part(tiles - 1)
+    before = wrapped[0]
+    for c in range(tiles):
+        fluxes, dh, ue = wrapped if c == tiles - 1 else lon_part(c)
+        cols = slice(128 * c, 128 * c + 128)
+        u, v = load(1, r, c), load(2, r, c)
+        vn = row_up(v, load(2, r + 8, c), 1, rows)
+        p, q, s = face_terms((0.5 * b) * (v + vn))
+        tends = []
+        dn = None
+        for k, m in enumerate(masses):
+            prv, cur, nxt = load(m, r - 8, c), load(m, r, c), load(m, r + 8, c)
+            n, so = row_up(cur, nxt, 1, rows), row_down(cur, prv, 1, rows)
+            if m == 0:
+                dn = n - so
+            up = p * cur + q * n - s * (so + row_up(cur, nxt, 2, rows))
+            tends.append(
+                lane_down(fluxes[k], before[k], 1, lanes)
+                - fluxes[k]
+                + (row_down(up, carry[k, :, cols], 1, rows) - up)
+            )
+            carry[k, :, cols] = up
+        before = fluxes
+        au, bv = half_a * u, (0.5 * b) * v
+        du = row_up(u, load(1, r + 8, c), 1, rows) - row_down(u, load(1, r - 8, c), 1, rows)
+        dv = vn - row_down(v, load(2, r - 8, c), 1, rows)
+        tu = f * v - au * (ue - near(1, r, c, -1)) - bv * du - half_a * dh
+        tv = -(f * u) - au * (near(2, r, c, 1) - near(2, r, c, -1)) - bv * dv - (0.5 * b) * dn
+        emit(c, [tends[0], tu, tv] + tends[1:])
 
 
 def widen(x, width, east, west, east_shift, west_shift):
@@ -138,13 +194,14 @@
     lev, n_rows, cells, width, count, bands = geo
     left, right = refs[0:5], refs[5:10]
     fields = refs[10:15]
-    par, lat_c, cuts, uh, ul, gh, gl = refs[15:22]
-    out_east, out_west, out_north, out_south, out_coef = refs[22:27]
+    courant, rotate, cuts, lat_c, uh, ul = refs[15:21]
+    in_hbm = refs[21:25]
+    out_east, out_west, out_north, out_south, out_coef = refs[25:30]
     (
         send_w, send_e, got_e, got_w, edge_n, edge_s, send_n, send_s, got_n, got_s,
-        cap_raw, cap, cap_t, comp, mid_in, mid_out, coef,
+        cap_raw, cap, cap_t, carry, gh, gl, th, tl, comp, mid_in, mid_out, coef,
         in_sem, lon_send, lon_recv, lat_send, lat_recv, a_send, a_recv, b_send, b_recv,
-    ) = refs[27:]
+    ) = refs[30:]
     me = lax.axis_index("lon")
     band = lax.axis_index("lat")
     has_n = band > 0
@@ -185,7 +242,11 @@
         )
         for k in range(3)
     ]
-    for copy in loads + cap_loads:
+    table_loads = [
+        pltpu.make_async_copy(src, dst, in_sem.at[13 + k])
+        for k, (src, dst) in enumerate(zip(in_hbm, (gh, gl, th, tl)))
+    ]
+    for copy in loads + cap_loads + table_loads:
         copy.start()
 
     ids = lax.broadcasted_iota(jnp.int32, (n_rows, 128), 1)
@@ -246,9 +307,12 @@
     out_east[...] = got_e[...]
     out_west[...] = got_w[...]
 
+    for copy in table_loads:
+        copy.wait()
+
     @pl.when(is_cap)
     def _():
-        rows = row_ids(width)
+        rows, lanes = tile_ids()
         b = lat_c[0]
         halo_row = pl.multiple_of(cap_row, 8)
         for k in range(3):
@@ -266,30 +330,26 @@
         first = jnp.where(band == 0, 8, 16)
 
         def level_body(level, _):
-            def load(m, r):
-                return cap[m, level, pl.ds(pl.multiple_of(r, 8), 8), :]
-
-            def body(c, carry):
-                r = first + 8 * c
-                pr = pl.multiple_of(jnp.where(band == 0, 0, n_rows - CAP) + 8 * c, 8)
-                a = par[pl.ds(pr, 8), 0:1]
-                f = par[pl.ds(pr, 8), 1:2]
-                tends, tu, tv, fluxes = chunk(load, r, a, f, b, (0,), carry, rows)
-                dst = pl.multiple_of(8 * c, 8)
-                cap_t[0, level, pl.ds(dst, 8), :] = tends[0]
-                cap_t[1, level, pl.ds(dst, 8), :] = tu
-                cap_t[2, level, pl.ds(dst, 8), :] = tv
-                return fluxes
-
-            v, vn = load(2, first - 8), load(2, first)
-            p, q, s = face_terms((0.5 * b) * (v + row_up(v, vn, 1, rows)))
-            cur, nxt = load(0, first - 8), load(0, first)
-            before = (
-                p * cur
-                + q * row_up(cur, nxt, 1, rows)
-                - s * (row_down(cur, cur, 1, rows) + row_up(cur, nxt, 2, rows))
-            )
-            lax.fori_loop(0, CAP // 8, body, [before])
+            def load(m, r, c):
+                at = pl.multiple_of(r, 8)
+                return cap[m, level, pl.ds(at, 8), 128 * c : 128 * c + 128]
+
+            first_carry(load, first - 8, b, (0,), width // 128, carry)
+
+            def body(i, _):
+                pr = jnp.where(band == 0, 0, n_rows - CAP) + 8 * i
+                a, f = eight_rows(courant, pr, rows), eight_rows(rotate, pr, rows)
+                dst = pl.multiple_of(8 * i, 8)
+
+                def emit(c, tends):
+                    for k in range(3):
+                        cap_t[k, level, pl.ds(dst, 8), 128 * c : 128 * c + 128] = tends[k]
+
+                near = rolled(load, width // 128)
+                chunk(load, near, first + 8 * i, a, f, b, (0,), width // 128, carry, emit)
+                return 0
+
+            lax.fori_loop(0, CAP // 8, body, 0, unroll=2)
             return 0
 
         lax.fori_loop(0, lev, level_body, 0)
@@ -309,20 +369,25 @@
         mid_in[me] = comp[me]
         for copy in first_sends:
             copy.wait()
-        spectra = None
-        for s in range(count):
-            part = pl.ds(s * RANK, RANK)
-            term = dot3(mid_in[s], gh[part, :], gl[part, :])
-            spectra = term if spectra is None else spectra + term
+        gathered = jnp.concatenate([mid_in[s] for s in range(count)], 1)
+        spectra = dot3(gathered, gh[...], gl[...])
         modes = lax.broadcasted_iota(jnp.int32, (owned, 2 * KEEP), 1)
         modes = jnp.where(modes >= KEEP, modes - KEEP, modes)
         full = cells * count
         weight = jnp.where(modes == 0, 1.0 / full, 2.0 / full).astype(jnp.float32)
-        limit = cuts[pl.ds(pl.multiple_of(me * owned, 8), owned), 0:1]
-        spectra = jnp.where(modes.astype(jnp.float32) <= limit, spectra * weight, 0.0)
+        mode_rows = lax.broadcasted_iota(jnp.int32, (8, 2 * KEEP), 0)
+        base = jnp.where(band == 0, 0, n_rows - CAP)
+        limit = jnp.concatenate(
+            [
+                eight_rows(cuts, base + lax.rem(me * owned + 8 * g, CAP), mode_rows)
+                for g in range(owned // 8)
+            ],
+            0,
+        )
+        spectra = jnp.where(modes <= limit, spectra * weight, 0.0)
+        spread = dot3(spectra, th[...], tl[...])
         for s in range(count):
-            part = pl.ds(s * RANK, RANK)
-            mid_out[s] = dot3(spectra, gh[part, :], gl[part, :], 1)
+            mid_out[s] = spread[:, RANK * s : RANK * s + RANK]
         second_sends = [send(mid_out, coef, b_send, b_recv, j) for j in range(1, count)]
         for copy in second_sends:
             copy.start()
@@ -360,23 +425,28 @@
 def step_kernel(geo, *refs):
     lev, n_rows, cells, width, count, bands = geo
     fields = refs[0:5]
-    par, lat_c, east, west, north, south, coef, wh, wl = refs[5:14]
-    outs = refs[14:19]
-    pad = refs[19]
+    courant, rotate, mask, lat_c, east, west, north, south, coef, wh, wl, moves = refs[5:17]
+    outs = refs[17:22]
+    pad, ahead, beyond, carry = refs[22:26]
     level = pl.program_id(0)
     band = lax.axis_index("lat")
     last = width - 128
     e = cells - last
-    rows = row_ids(width)
+    rows, lanes = tile_ids()
     b = lat_c[0]
+    tiles = width // 128
+    zeros = jnp.zeros((8, 128), jnp.float32)
     for k in range(5):
-        pad[k, 0:8, :] = jnp.zeros((8, width), jnp.float32)
-        pad[k, n_rows + 8 : n_rows + 16, :] = jnp.zeros((8, width), jnp.float32)
-        pad[k, 6:8, :cells] = north[0, 2 * k : 2 * k + 2, :]
-        pad[k, n_rows + 8 : n_rows + 10, :cells] = south[0, 2 * k : 2 * k + 2, :]
+        for c in range(tiles):
+            stop = min(cells, 128 * c + 128)
+            wide = stop - 128 * c
+            pad[k, c, 0:8, :] = zeros
+            pad[k, c, n_rows + 8 : n_rows + 16, :] = zeros
+            pad[k, c, 6:8, :wide] = north[0, 2 * k : 2 * k + 2, 128 * c : stop]
+            pad[k, c, n_rows + 8 : n_rows + 10, :wide] = south[0, 2 * k : 2 * k + 2, 128 * c : stop]
     for k in (3, 4):
         for r in (0, n_rows + 8):
-            pad[k, r : r + 8, :] = pad[k, r : r + 8, :] * pad[0, r : r + 8, :]
+            pad[k, :, r : r + 8, :] = pad[k, :, r : r + 8, :] * pad[0, :, r : r + 8, :]
 
     def fill(c, _):
         r = pl.multiple_of(8 * c, 8)
@@ -393,45 +463,68 @@
                 thick = body, tail
             if k >= 3:
                 body, tail = body * thick[0], tail * thick[1]
-            pad[k, pl.ds(to, 8), :last] = body
-            pad[k, pl.ds(to, 8), last:] = tail
+            for t in range(tiles - 1):
+                pad[k, t, pl.ds(to, 8), :] = body[:, 128 * t : 128 * t + 128]
+            pad[k, tiles - 1, pl.ds(to, 8), :] = tail
         return 0
 
-    lax.fori_loop(0, n_rows // 8, fill, 0)
-
-    def load(m, r):
-        return pad[m, pl.ds(pl.multiple_of(r, 8), 8), :]
+    lax.fori_loop(0, n_rows // 8, fill, 0, unroll=4)
+
+    def load(m, r, c):
+        return pad[m, c, pl.ds(pl.multiple_of(r, 8), 8), :]
+
+    depth = n_rows + 16
+    for k in range(5):
+        flat = pad[k].reshape(tiles * depth, 128)
+        moved = jnp.dot(
+            jnp.concatenate(halves(flat), 1),
+            moves[1 if k in (1, 2) else 0],
+            preferred_element_type=jnp.float32,
+        )
+        ahead[k] = moved[:, :128].reshape(tiles, depth, 128)
+        beyond[k] = moved[:, 128:].reshape(tiles, depth, 128)
+
+    by_roll = rolled(load, tiles)
+
+    def near(m, r, c, k):
+        wind = m in (1, 2)
+        if k == -1 and not wind:
+            return by_roll(m, r, c, k)
+        at = pl.ds(pl.multiple_of(r, 8), 8)
+        east, west = (c + 1) % tiles, (c + tiles - 1) % tiles
+        if k == 1:
+            return jnp.where(lanes < 127, ahead[m, c, at, :], ahead[m, east, at, :])
+        if k == 2:
+            return jnp.where(lanes < 126, beyond[m, c, at, :], beyond[m, east, at, :])
+        return jnp.where(lanes > 0, beyond[m, c, at, :], beyond[m, west, at, :])
 
     masses = (0, 3, 4)
-    v, vn = load(2, 0), load(2, 8)
-    p, q, s = face_terms((0.5 * b) * (v + row_up(v, vn, 1, rows)))
-    before = []
-    for m in masses:
-        cur, nxt = load(m, 0), load(m, 8)
-        before.append(
-            p * cur
-            + q * row_up(cur, nxt, 1, rows)
-            - s * (row_down(cur, cur, 1, rows) + row_up(cur, nxt, 2, rows))
-        )
-
-    def body(c, carry):
-        r = 8 * c + 8
-        src = pl.multiple_of(8 * c, 8)
-        a = par[pl.ds(src, 8), 0:1]
-        f = par[pl.ds(src, 8), 1:2]
-        tends, tu, tv, fluxes = chunk(load, r, a, f, b, masses, carry, rows)
-        for k, t in zip(range(5), (tends[0], tu, tv, tends[1], tends[2])):
-            outs[k][0, pl.ds(src, 8), :] = (load(k, r) + t)[:, :cells]
-        return fluxes
-
-    lax.fori_loop(0, n_rows // 8, body, before)
+    first_carry(load, 0, b, masses, tiles, carry)
+
+    def body(i, _):
+        r = 8 * i + 8
+        src = pl.multiple_of(8 * i, 8)
+        a, f = eight_rows(courant, src, rows), eight_rows(rotate, src, rows)
+
+        def emit(c, tends):
+            stop = min(cells, 128 * c + 128)
+            for k in range(5):
+                new = load(k, r, c) + tends[k]
+                outs[k][0, pl.ds(src, 8), 128 * c : stop] = new[:, : stop - 128 * c]
+
+        chunk(load, near, r, a, f, b, masses, tiles, carry, emit)
+        return 0
+
+    lax.fori_loop(0, n_rows // 8, body, 0, unroll=2)
 
     @pl.when(jnp.logical_or(band == 0, band == bands - 1))
     def _():
         start = pl.multiple_of(jnp.where(band == 0, 0, n_rows - CAP), 8)
         flat = coef[...].reshape(3 * CAP, RANK)
         smooth = dot3(flat, wh[...], wl[...])
-        chosen = par[pl.ds(start, CAP), 2:3] == 1.0
+        wide_rows = lax.broadcasted_iota(jnp.int32, (8, cells), 0)
+        flags = [eight_rows(mask, start + 8 * g, wide_rows) for g in range(CAP // 8)]
+        chosen = jnp.concatenate(flags, 0) == 1
         for k in range(3):
             new = fields[k][0, pl.ds(start, CAP), :] + smooth[CAP * k : CAP * k + CAP, :cells]
             old = outs[k][0, pl.ds(start, CAP), :]
@@ -444,16 +537,10 @@
     bands = lax.axis_size("lat")
     width = (cells + 4 + 127) // 128 * 128
     geo = (lev, n_rows, cells, width, count, bands)
-    uh, ul, wh, wl, gh, gl = (jnp.asarray(t) for t in tables(cells, count, width))
+    uh, ul, wh, wl, gh, gl, th, tl = (jnp.asarray(t) for t in tables(cells, count, width))
     fields = (thick, uwind, vwind, theta, moist)
-    par = jnp.stack(
-        [lon_courant, coriolis, (cap_mask == 1).astype(jnp.float32)], 1
-    )
-    cap_cuts = jnp.where(
-        lax.axis_index("lat") == 0, cutoffs[:CAP], cutoffs[n_rows - CAP :]
-    ).astype(jnp.float32)
-    cuts = jnp.tile(cap_cuts, 3 * lev)[:, None]
     lat_c = lat_courant.reshape(1)
+    moves = jnp.asarray(shift_tables())
 
     whole = lambda shape: pl.BlockSpec(shape, lambda i: (0,) * len(shape))
     smem = pl.BlockSpec(memory_space=pltpu.SMEM)
@@ -475,8 +562,9 @@
         in_specs=[edge(0)] * 5
         + [edge(cells // 128)] * 5
         + [pl.BlockSpec(memory_space=pl.ANY)] * 5
-        + [whole(par.shape), smem, whole(cuts.shape)]
-        + [whole(t.shape) for t in (uh, ul, gh, gl)],
+        + [smem] * 4
+        + [whole(uh.shape)] * 2
+        + [pl.BlockSpec(memory_space=pl.ANY)] * 4,
         out_specs=(
             whole((n_rows, 128)),
             whole((n_rows, 128)),
@@ -491,16 +579,21 @@
             pltpu.VMEM((3, lev, CAP + 8, cells), f32),
             pltpu.VMEM((3, lev, CAP + 24, width), f32),
             pltpu.VMEM((3, lev, CAP, width), f32),
+            pltpu.VMEM((1, 8, width), f32),
+            pltpu.VMEM(gh.shape, jnp.bfloat16),
+            pltpu.VMEM(gl.shape, jnp.bfloat16),
+            pltpu.VMEM(th.shape, jnp.bfloat16),
+            pltpu.VMEM(tl.shape, jnp.bfloat16),
         ]
         + [pltpu.VMEM((count, owned, RANK), f32)] * 4
-        + [dma((13,))]
+        + [dma((17,))]
         + [dma((2,))] * 4
         + [dma((count,))] * 4,
         compiler_params=pltpu.CompilerParams(
             collective_id=0, has_side_effects=True, vmem_limit_bytes=VMEM_LIMIT
         ),
         name="exchange",
-    )(*fields, *fields, *fields, par, lat_c, cuts, uh, ul, gh, gl)
+    )(*fields, *fields, *fields, lon_courant, coriolis, cutoffs, lat_c, uh, ul, gh, gl, th, tl)
 
     by_level = lambda shape: pl.BlockSpec(
         (1,) + shape, lambda i: (i,) + (0,) * len(shape)
@@ -511,15 +604,20 @@
         grid=(lev,),
         out_shape=tuple(jax.ShapeDtypeStruct((lev, n_rows, cells), f32) for _ in range(5)),
         in_specs=[by_level((n_rows, cells))] * 5
-        + [whole(par.shape), smem, whole((n_rows, 128)), whole((n_rows, 128))]
+        + [smem] * 4
+        + [whole((n_rows, 128))] * 2
         + [by_level((10, cells))] * 2
         + [pl.BlockSpec((3, 1, CAP, RANK), lambda i: (0, i, 0, 0))]
-        + [whole(wh.shape)] * 2,
+        + [whole(wh.shape)] * 2
+        + [whole(moves.shape)],
         out_specs=[by_level((n_rows, cells))] * 5,
-        scratch_shapes=[pltpu.VMEM((5, n_rows + 16, width), f32)],
+        scratch_shapes=[
+            *[pltpu.VMEM((5, width // 128, n_rows + 16, 128), f32)] * 3,
+            pltpu.VMEM((3, 8, width), f32),
+        ],
         compiler_params=pltpu.CompilerParams(vmem_limit_bytes=VMEM_LIMIT),
         name="substep",
-    )(*fields, par, lat_c, east, west, north, south, coef, wh, wl)
+    )(*fields, lon_courant, coriolis, cap_mask, lat_c, east, west, north, south, coef, wh, wl, moves)
 
 
 def solution(mesh):

time: 71.4 us -> 55 us (0.77)
  Pallas kernels: 66 us -> 53.5 us
  other arithmetic: 2.21 us -> 0 us
  local copies, waits for them, and re-layouts: 1.64 us -> 0 us
    pallas_call x1, Pallas kernels: 34.5 us -> 24.5 us  [local(): pl.pallas_call(functools.partial(step_kernel, geo), grid=(lev,), out_shap...]
    pallas_call x1, Pallas kernels: 31.5 us -> 29 us  [local(): pl.pallas_call(functools.partial(exchange_kernel, geo), grid=(1,), out_sh...]
    another operation x3 -> x0, local copies, waits for them, and re-layouts: 1.64 us -> none  [the longest x2 0.88 us: local(): cuts = jnp.tile(cap_cuts, 3 * lev)[:, None]]
    another operation x2 -> x0, other arithmetic: 1.38 us -> none  [local(): jnp.stack([lon_courant, coriolis, (cap_mask == 1).astype(jnp.float32)], 1)]
    convert_element_type x1 -> x0, other arithmetic: 0.83 us -> none  [local(): cap_cuts = jnp.where(lax.axis_index('lat') == 0, cutoffs[:CAP], cutoffs[n...]
where the time goes in v1:
time: 55 us; the launch traced here: 54.8 us
  Pallas kernels  53.5 us (97%)
  between operations  1.29 us (2%)
    pallas_call x1, Pallas kernels, local(): pl.pallas_call(functools.partial(exchange_kernel, geo), grid=(1,), out_sh...  29 us
    pallas_call x1, Pallas kernels, local(): pl.pallas_call(functools.partial(step_kernel, geo), grid=(lev,), out_shap...  24.5 us

profile of v1, /device:TPU:0, one launch (start us, length us, event | category | flops | bytes accessed | tf_op | source)
XLA Modules:
  0.0 54.8 jit_solution(1436308153637614889)
XLA Ops:
  1.3 29.0 %exchange.1 = (f32[192,128]{1,0:T(8,128)}, f32[192,128]{1,0:T(8,128)}, f32[4,10,720]{2,1,0:T(8,128)}, f32[4,10,720]{2,1,0:T(8,128)}, f32[384,128]{1,0:T(8,128)}) custom-call(f32[4,192,720]{2,1,0:T(8,128)} %refs_0_.3, f32[4,192,720]{2,1,0:T(8,128)} %refs_1_.3, f32[4,192,720]{2,1,0:T(8,128)} %refs_2_.3, f32[4,192,720]{2,1,0:T(8,128)} %refs_3_.3, ...), custom_call_target="tpu_custom_call" | custom-call | tf_op jit(solution)/shard_map/exchange/pallas_call | solution.py:552
  30.3 24.5 %substep.1 = (f32[4,192,720]{2,1,0:T(8,128)}, f32[4,192,720]{2,1,0:T(8,128)}, f32[4,192,720]{2,1,0:T(8,128)}, f32[4,192,720]{2,1,0:T(8,128)}, f32[4,192,720]{2,1,0:T(8,128)}) custom-call(f32[4,192,720]{2,1,0:T(8,128)} %refs_0_.3, f32[4,192,720]{2,1,0:T(8,128)} %refs_1_.3, f32[4,192,720]{2,1,0:T(8,128)} %refs_2_.3, f32[4,192,720]{2,1,0:T(8,128)} %refs_3_.3, ...), custom_call_target="tpu_custom_call" | custom-call | tf_op jit(solution)/shard_map/substep/pallas_call | solution.py:602

commit v2 on v1

--- a/solution.py
+++ b/solution.py
@@ -185,9 +185,16 @@
     )
     ids = lax.broadcasted_iota(jnp.int32, (x.shape[0], 128), 1)
     e = cells - last
-    tail = jnp.where((ids >= e) & (ids < e + 2), pltpu.roll(east, east_shift, 1), tail)
-    tail = jnp.where(ids >= 126, pltpu.roll(west, west_shift, 1), tail)
+    moved = pltpu.roll(east, east_shift, 1)
+    tail = jnp.where((ids >= e) & (ids < e + 2), moved, tail)
+    if west is not None:
+        moved = pltpu.roll(west, west_shift, 1)
+    tail = jnp.where(ids >= 126, moved, tail)
     return x[:, :last], tail
+
+
+def west_offset(e, lev):
+    return 126 - e if 126 - e >= 10 * lev and 126 - e + 10 * lev <= 128 else 0
 
 
 def exchange_kernel(geo, *refs):
@@ -210,6 +217,7 @@
     last = width - 128
     e = cells - last
     owned = 3 * lev * CAP // count
+    gap = west_offset(e, lev)
 
     barrier = pltpu.get_barrier_semaphore()
     for j in range(1, count):
@@ -249,32 +257,34 @@
     for copy in loads + cap_loads + table_loads:
         copy.start()
 
+    to_west = pltpu.make_async_remote_copy(
+        src_ref=send_w, dst_ref=got_e, send_sem=lon_send.at[0], recv_sem=lon_recv.at[0],
+        device_id={"lon": lax.rem(me + count - 1, count)},
+    )
+    to_east = pltpu.make_async_remote_copy(
+        src_ref=send_e, dst_ref=got_w, send_sem=lon_send.at[1], recv_sem=lon_recv.at[1],
+        device_id={"lon": lax.rem(me + 1, count)},
+    )
     ids = lax.broadcasted_iota(jnp.int32, (n_rows, 128), 1)
     west_edge = jnp.zeros((n_rows, 128), jnp.float32)
     east_edge = jnp.zeros((n_rows, 128), jnp.float32)
-    for k in range(5):
-        for level in range(lev):
+    for level in range(lev):
+        for k in range(5):
             at = 2 * (5 * level + k)
             here = (ids >= at) & (ids < at + 2)
             west_edge = jnp.where(here, pltpu.roll(left[k][level], at, 1), west_edge)
+    send_w[...] = west_edge
+    greeted = count - 1 + jnp.where(has_n, 1, 0) + jnp.where(has_s, 1, 0)
+    pl.semaphore_wait(barrier, greeted)
+    to_west.start()
+    for level in range(lev):
+        for k in range(5):
+            at = 2 * (5 * level + k) + gap
+            here = (ids >= at) & (ids < at + 2)
             east_edge = jnp.where(
                 here, pltpu.roll(right[k][level], (at - (e - 2)) % 128, 1), east_edge
             )
-    send_w[...] = west_edge
     send_e[...] = east_edge
-
-    greeted = count - 1 + jnp.where(has_n, 1, 0) + jnp.where(has_s, 1, 0)
-    pl.semaphore_wait(barrier, greeted)
-
-    to_west = pltpu.make_async_remote_copy(
-        src_ref=send_w, dst_ref=got_e, send_sem=lon_send.at[0], recv_sem=lon_recv.at[0],
-        device_id={"lon": lax.rem(me + count - 1, count)},
-    )
-    to_east = pltpu.make_async_remote_copy(
-        src_ref=send_e, dst_ref=got_w, send_sem=lon_send.at[1], recv_sem=lon_recv.at[1],
-        device_id={"lon": lax.rem(me + 1, count)},
-    )
-    to_west.start()
     to_east.start()
 
     for copy in loads:
@@ -304,6 +314,8 @@
         copy.wait()
     to_west.wait()
     to_east.wait()
+    if gap:
+        got_e[...] = got_e[...] + got_w[...]
     out_east[...] = got_e[...]
     out_west[...] = got_w[...]
 
@@ -320,7 +332,8 @@
                 at = 2 * (5 * level + k)
                 body, tail = widen(
                     cap_raw[k, level], width,
-                    got_e[pl.ds(halo_row, CAP + 8), :], got_w[pl.ds(halo_row, CAP + 8), :],
+                    got_e[pl.ds(halo_row, CAP + 8), :],
+                    None if gap else got_w[pl.ds(halo_row, CAP + 8), :],
                     (e - at) % 128, (126 - at) % 128,
                 )
                 cap[k, level, 0:8, :] = jnp.zeros((8, width), jnp.float32)
@@ -451,7 +464,8 @@
     def fill(c, _):
         r = pl.multiple_of(8 * c, 8)
         to = pl.multiple_of(8 * c + 8, 8)
-        ea, we = east[pl.ds(r, 8), :], west[pl.ds(r, 8), :]
+        ea = east[pl.ds(r, 8), :]
+        we = None if west_offset(e, lev) else west[pl.ds(r, 8), :]
         thick = None
         for k in range(5):
             at = 2 * (5 * level + k)

time: 55 us -> 54.4 us (0.989)
  Pallas kernels: 53.5 us -> 52.9 us
where the time goes in v2:
time: 54.4 us; the launch traced here: 54.2 us
  Pallas kernels  52.9 us (97%)
  between operations  1.29 us (2%)
    pallas_call x1, Pallas kernels, local(): pl.pallas_call(functools.partial(exchange_kernel, geo), grid=(1,), out_sh...  28.9 us
    pallas_call x1, Pallas kernels, local(): pl.pallas_call(functools.partial(step_kernel, geo), grid=(lev,), out_shap...  24 us

profile of v2, /device:TPU:0, one launch (start us, length us, event | category | flops | bytes accessed | tf_op | source)
XLA Modules:
  0.0 54.2 jit_solution(17337274679316325586)
XLA Ops:
  1.3 28.9 %exchange.1 = (f32[192,128]{1,0:T(8,128)}, f32[192,128]{1,0:T(8,128)}, f32[4,10,720]{2,1,0:T(8,128)}, f32[4,10,720]{2,1,0:T(8,128)}, f32[384,128]{1,0:T(8,128)}) custom-call(f32[4,192,720]{2,1,0:T(8,128)} %refs_0_.3, f32[4,192,720]{2,1,0:T(8,128)} %refs_1_.3, f32[4,192,720]{2,1,0:T(8,128)} %refs_2_.3, f32[4,192,720]{2,1,0:T(8,128)} %refs_3_.3, ...), custom_call_target="tpu_custom_call" | custom-call | tf_op jit(solution)/shard_map/exchange/pallas_call | solution.py:566
  30.2 24.0 %substep.1 = (f32[4,192,720]{2,1,0:T(8,128)}, f32[4,192,720]{2,1,0:T(8,128)}, f32[4,192,720]{2,1,0:T(8,128)}, f32[4,192,720]{2,1,0:T(8,128)}, f32[4,192,720]{2,1,0:T(8,128)}) custom-call(f32[4,192,720]{2,1,0:T(8,128)} %refs_0_.3, f32[4,192,720]{2,1,0:T(8,128)} %refs_1_.3, f32[4,192,720]{2,1,0:T(8,128)} %refs_2_.3, f32[4,192,720]{2,1,0:T(8,128)} %refs_3_.3, ...), custom_call_target="tpu_custom_call" | custom-call | tf_op jit(solution)/shard_map/substep/pallas_call | solution.py:616
